TPU v7x, 256 devices: a whole 4x4x8 slice. The times are simulated.
256 devices in a mesh: keys: 64 (over z, y, core), tiles: 4 (over x).
Axes of the slice: x: 4, y: 4, z: 8, core: 2. Of those that a mesh axis runs over, the one named last changes fastest.
Arguments:
- fact_store: int32 [1048576], P(('keys', 'tiles')), may hold values from 0 to 16383, as said below
- fact_item: int32 [1048576], P(('keys', 'tiles')), may hold values from 0 to 4095, as said below
- store_count: int32 [16384], P('keys'), may hold values from 1 to 64, as said below
- store_table: bfloat16 [16384, 1024], P('keys'), may hold values from -6 to 6
- item_table: bfloat16 [4096, 1024], P('tiles'), may hold values from -6 to 6
Outputs:
- gram_left: float32 [1024, 2048], P('keys', 'tiles')
- gram_items: float32 [1024, 1024], P('keys', 'tiles')
Inputs may be any that keep to these rules, and one draw needn't show every extreme that they name: `fact_store`: every fact row held by keys index g names a store of g * 256 to (g + 1) * 256 - 1. `fact_item`: every fact row held by tiles index t names an item of t * 1024 to (t + 1) * 1024 - 1. `store_count`: each a power of two.
All inputs are finite; a program needn't handle non-finite values.
Results may differ from a plain program's by a relative error of at most 0.0003.
Values sent between devices are 32-bit elements; how exact they have to be, the bound alone decides.
A program may use at most 64 MiB of HBM per device.

v0:
```python
import jax
import jax.numpy as jnp
from jax import lax
from jax.sharding import PartitionSpec as P


def shards(fact_store, fact_item, store_count, store_table, item_table):
    key_dev, width_a = store_table.shape
    item_dev, width_b = item_table.shape
    keys_count = lax.axis_size("keys")
    tiles_count = lax.axis_size("tiles")
    tile_index = lax.axis_index("tiles")
    local_store = fact_store - lax.axis_index("keys") * key_dev
    local_item = fact_item - tile_index * item_dev
    store_hit = lax.iota(jnp.int32, key_dev)[:, None] == local_store[None, :]
    weighted = jnp.where(store_hit, store_count[:, None], 0)
    row_weight = jnp.sum(weighted, axis=0)
    store_weight = jnp.sum(weighted, axis=1).astype(jnp.float32)
    item_rows = jnp.take(item_table, local_item, axis=0)
    aggregate = jnp.dot(
        weighted.astype(jnp.bfloat16), item_rows, preferred_element_type=jnp.float32
    )
    store_float = store_table.astype(jnp.float32)
    tile_width = (width_a + width_b) // tiles_count
    store_weight, aggregate = lax.psum((store_weight, aggregate), "tiles")
    combined = jnp.concatenate([store_weight[:, None] * store_float, aggregate], axis=1)
    tile_cols = lax.dynamic_slice_in_dim(combined, tile_index * tile_width, tile_width, 1)
    left_part = lax.psum_scatter(
        lax.dot_general(
            store_float,
            tile_cols,
            (((0,), (0,)), ((), ())),
            precision=lax.Precision.HIGHEST,
            preferred_element_type=jnp.float32,
        ),
        "keys",
        scatter_dimension=0,
        tiled=True,
    )
    group_total = jnp.sum(store_weight)
    row_block = width_b // keys_count
    item_hit = (local_item[:, None] == lax.iota(jnp.int32, item_dev)[None, :]).astype(jnp.bfloat16)
    item_weight = jnp.dot(
        row_weight.astype(jnp.bfloat16)[None, :], item_hit, preferred_element_type=jnp.float32
    )[0]
    item_weight, total = lax.psum((item_weight, group_total), "keys")
    left_cols = lax.dynamic_slice_in_dim(
        item_table, lax.axis_index("keys") * row_block, row_block, 1
    ).astype(jnp.float32)
    right_side = item_table.astype(jnp.float32) * item_weight[:, None]
    partial_rows = lax.dot_general(
        left_cols,
        right_side,
        (((0,), (0,)), ((), ())),
        precision=lax.Precision.HIGHEST,
        preferred_element_type=jnp.float32,
    )
    item_block = lax.psum_scatter(partial_rows, "tiles", scatter_dimension=1, tiled=True)
    return (left_part / total, item_block / total)


def solution(mesh):
    placed = (
        P(("keys", "tiles")),
        P(("keys", "tiles")),
        P("keys"),
        P("keys", None),
        P("tiles", None),
    )
    return jax.shard_map(
        shards,
        mesh=mesh,
        in_specs=placed,
        out_specs=(P("keys", "tiles"), P("keys", "tiles")),
        check_vma=False,
    )
```

profile of v0, /device:TPU:4, one launch (start us, length us, event | category | flops | bytes accessed | tf_op | source)
XLA Modules:
  0.0 356.4 jit_solution(1234094113621853639)
XLA Ops:
  7.2 0.0 all-reduce.3.cloned.1.call-start
  7.2 0.7 compare_and_fusion
  8.0 0.0 copy-start.2
  8.0 0.0 copy-start.3
  8.0 22.8 %gather_fusion = bf16[4096,1024]{1,0:T(8,128)(2,1)} fusion(bf16[1024,1024]{1,0:T(8,128)(2,1)} %param.9, s32[4096]{0:T(1024)S(1)} %fusion.16), kind=kCustom, calls=%fused_computation | custom fusion | bytes 16793600 | tf_op jit(solution)/shard_map/jit(_take)/gather | solution.py:19
  30.7 0.0 copy-done.2
  30.8 0.0 copy-done.3
  30.8 6.9 %fusion.2 = f32[256,1024]{1,0:T(8,128)} fusion(bf16[4096,1024]{1,0:T(8,128)(2,1)} %gather_fusion, pred[4096]{0:T(1024)(128)(4,1)S(1)} %get-tuple-element.12, s32[256]{0:T(256)S(1)} %copy-done.3, s32[4096]{0:T(1024)S(1)} %broadcast_subtract_fusion.1), kind=kOutput, calls=%fused_computation.4 | convolution fusion | flops 2154823680 | bytes 9458688 | tf_op jit(solution)/shard_map/dot_general | solution.py:20
  37.6 0.0 copy-start
  37.6 0.0 copy-start.1
  37.6 0.0 all-reduce.3.cloned.1.call-update
  37.7 0.0 reduce-scatter.5.cloned.1.call-start
  37.7 0.9 select_reduce_fusion
  38.7 8.3 %psum.28 = f32[256]{0:T(256)S(1)} all-reduce(f32[256]{0:T(256)S(1)} %convert_element_type.19), channel_id=1, replica_groups=mesh['keys'=64,'tiles'=4] {'tiles'}, use_global_device_ids=true, to_apply=%region_1.2 | all-reduce | flops 256 | bytes 2048 | tf_op jit(solution)/shard_map/psum | solution.py:25
  47.0 0.6 reduce_sum.28
  47.6 3.0 fusion
  50.6 132.4 %all-reduce = (f32[]{:T(128)}, f32[1024]{0:T(1024)S(1)}) all-reduce(f32[]{:T(128)} %reduce_sum.28, f32[1024]{0:T(1024)S(1)} %bitcast.6), channel_id=1, replica_groups=mesh['keys'=64,'tiles'=4] {'keys'}, use_global_device_ids=true, to_apply=%region_5.6 | all-reduce | flops 1025 | bytes 8200 | tf_op jit(solution)/shard_map/psum | solution.py:46
  183.0 0.0 copy-done
  183.0 2.4 fusion.5
  185.5 0.0 reduce-scatter.5.cloned.1.call-update
  185.5 0.0 reduce-scatter.7.cloned.1.call-start
  185.5 0.0 copy-done.1
  185.6 0.1 convert_multiply_fusion
  185.7 0.0 all-reduce.3.cloned.1.call-done
  185.7 2.3 convolution_bitcast_fusion
  188.0 1.9 copy.10
  189.9 0.0 reduce-scatter.7.cloned.1.call-update
  189.9 11.6 %reduce-scatter.5.cloned.1.call-done = f32[16,256]{1,0:T(8,128)} async-done(((f32[16,1024]{1,0:T(8,128)}), f32[16,256]{1,0:T(8,128)}) %reduce-scatter.5.cloned.1.call-update) | async-done | bytes 16400 | tf_op jit(solution)/shard_map/reduce_scatter | solution.py:58
  201.5 2.0 broadcast_divide_fusion.1
  203.5 144.2 %reduce-scatter.7.cloned.1.call-done = f32[16,512]{1,0:T(8,128)} async-done(((f32[1024,512]{1,0:T(8,128)}), f32[16,512]{1,0:T(8,128)}) %reduce-scatter.7.cloned.1.call-update) | async-done | bytes 32784
  347.6 0.9 copy.11
  348.5 0.7 broadcast_divide_fusion
  349.2 0.7 copy.9
  (5 shorter events, 0.0 us)
Async XLA Ops:
  7.2 178.6 %all-reduce.3.cloned.1.call-start = ((), (), s32[]{:S(2)}) async-start(), calls=%async_computation.2 | async-start | bytes 2097152 | tf_op jit(solution)/shard_map/psum | solution.py:25
  8.0 22.8 %copy-start.2 = (s32[4096]{0:T(1024)S(1)}, s32[4096]{0:T(1024)}, u32[]{:S(2)}) copy-start(s32[4096]{0:T(1024)} %param.5) | copy-start | bytes 49156
  8.0 22.8 %copy-start.3 = (s32[256]{0:T(256)S(1)}, s32[256]{0:T(256)}, u32[]{:S(2)}) copy-start(s32[256]{0:T(256)} %param.7) | copy-start | bytes 3076
  37.6 145.4 %copy-start = (bf16[1024,1024]{1,0:T(8,128)(2,1)S(1)}, bf16[1024,1024]{1,0:T(8,128)(2,1)}, u32[]{:S(2)}) copy-start(bf16[1024,1024]{1,0:T(8,128)(2,1)} %param.9) | copy-start | bytes 6291460
  37.6 147.9 %copy-start.1 = (bf16[256,1024]{1,0:T(8,128)(2,1)S(1)}, bf16[256,1024]{1,0:T(8,128)(2,1)}, u32[]{:S(2)}) copy-start(bf16[256,1024]{1,0:T(8,128)(2,1)} %param.8) | copy-start | bytes 1572868
  37.7 163.8 %reduce-scatter.5.cloned.1.call-start = ((), (), s32[]{:S(2)}) async-start(), calls=%async_computation.3 | async-start | bytes 81920 | tf_op jit(solution)/shard_map/reduce_scatter | solution.py:58
  185.5 162.1 %reduce-scatter.7.cloned.1.call-start = ((), (), s32[]{:S(2)}) async-start(), calls=%async_computation.4 | async-start | bytes 2129920
Sparse Core Ops, SparseCore 0:
  37.8 53.3 all-reduce.2
  185.6 15.8 reduce-scatter.4
  205.6 142.0 reduce-scatter.6
where the time goes:
time: 357 us; the launch traced here: 356 us
  waiting for transfers between devices  156 us (44%)
  blocking collectives  141 us (39%)
  local copies, waits for them, and re-layouts  26.3 us (7%)
  matrix products  14.6 us (4%)
  between operations  13.8 us (4%)
  other arithmetic  5.07 us (1%)
    unnamed x4, waiting for transfers between devices  144 us
    psum x1, blocking collectives, shards(): item_weight, total = lax.psum((item_weight, group_total), 'keys')  132 us
    gather x1, local copies, waits for them, and re-layouts, shards(): item_rows = jnp.take(item_table, local_item, axis=0)  22.8 us
    reduce_scatter x1, waiting for transfers between devices, shards(): lax.psum_scatter(partial_rows, 'tiles', scatter_dimension=1, tiled=True)  11.6 us
    psum x1, blocking collectives, shards(): store_weight, aggregate = lax.psum((store_weight, aggregate), 'tiles')  8.33 us
  transfers between devices with their start and end apart: 3, of which 2 were waited for; matrix products, arithmetic and copies ran while one was open for 4% of the time, Pallas kernels for 0%

commit v1 on v0

v1 whole, which is shorter than its diff:
```python
import functools

import jax
import jax.numpy as jnp
from jax import lax
from jax.experimental import pallas as pl
from jax.experimental.pallas import tpu as pltpu
from jax.sharding import PartitionSpec as P

MESH = pl.DeviceIdType.MESH
F32 = jnp.float32
BF16 = jnp.bfloat16
CORES = 2
LANES = 128


def nt_dot(a, b):
    return lax.dot_general(a, b, (((1,), (1,)), ((), ())), preferred_element_type=F32)


def dot(a, b):
    return jnp.dot(a, b, preferred_element_type=F32)


def split(x, axis):
    high = x.astype(BF16)
    low = (x - high.astype(F32)).astype(BF16)
    return jnp.concatenate([high, low], axis=axis)


def kernel(
    dims,
    fs_ref, fi_ref, sc_ref, s_hbm, i_hbm,
    left_ref, gram_ref,
    s_ref, i_ref, in_sem,
    counts, pairs, st_ref, scaled,
    n_part, n_recv, n_send_sem, n_recv_sem,
    a_part, a_recv, a_send_sem, a_recv_sem,
    q_part, q_recv, q_send_sem, q_recv_sem,
    y_part, y_recv, y_send_sem, y_recv_sem,
    z_part, z_recv, z_send_sem, z_recv_sem,
    w_part, w_recv, w_send_sem, w_recv_sem,
    g_part, g_recv, g_send_sem, g_recv_sem,
):
    X, Y, Z, key_dev, item_dev, cb, rows = dims
    g = lax.axis_index("keys")
    t = lax.axis_index("tiles")
    c = g % CORES
    y = (g // CORES) % Y
    z = g // (CORES * Y)

    def key(z_at, y_at, c_at):
        return (z_at * Y + y_at) * CORES + c_at

    barrier = pltpu.get_barrier_semaphore()
    greeted = 0
    for dx in range(X):
        for dz in range(Z):
            if dx or dz:
                pl.semaphore_signal(
                    barrier, inc=1, device_id=(key((z + dz) % Z, y, c), (t + dx) % X), device_id_type=MESH
                )
                greeted += 1
    for dy in range(1, Y):
        pl.semaphore_signal(barrier, inc=1, device_id=(key(z, (y + dy) % Y, c), t), device_id_type=MESH)
        greeted += 1
    pl.semaphore_signal(barrier, inc=1, device_id=(key(z, y, 1 - c), t), device_id_type=MESH)
    greeted += 1

    load_i = pltpu.make_async_copy(i_hbm, i_ref, in_sem.at[0])
    load_s = pltpu.make_async_copy(s_hbm, s_ref, in_sem.at[1])
    load_i.start()
    load_s.start()

    half = item_dev // 2
    local_store = fs_ref[...] - g * key_dev
    local_item = fi_ref[...] - t * item_dev
    upper = jnp.where(local_item >= half, 1, 0)
    u = (upper * key_dev + local_store - 256).astype(F32)
    v = (local_item - upper * half - 256).astype(F32)
    iota = (lax.broadcasted_iota(jnp.int32, (512, LANES), 0) - 256).astype(F32).astype(BF16)
    iota = iota.reshape(32, 16, LANES)

    def hot(row):
        row = jnp.broadcast_to(row, (16, LANES)).astype(BF16)
        return jnp.where(iota == row[None], jnp.ones((), BF16), jnp.zeros((), BF16)).reshape(512, LANES)

    per = 8
    for step in range(fs_ref.shape[0] // per):
        at = range(step * per, step * per + per)
        hot_u = jnp.concatenate([hot(u[r : r + 1]) for r in at], axis=1)
        hot_v = jnp.concatenate([hot(v[r : r + 1]) for r in at], axis=1)
        part = nt_dot(hot_u, hot_v)
        if step == 0:
            counts[...] = part
        else:
            counts[...] += part
    pairs[:, :half] = split(counts[:key_dev], 0)
    pairs[:, half:] = split(counts[key_dev:], 0)

    pl.semaphore_wait(barrier, greeted)

    def x_copy(src, dst, send, recv, k):
        return pltpu.make_async_remote_copy(
            src_ref=src, dst_ref=dst, send_sem=send, recv_sem=recv,
            device_id=(g, (t + k) % X), device_id_type=MESH,
        )

    ones = jnp.ones((8, item_dev), BF16)
    row = nt_dot(ones, pairs[...])
    n_part[...] = row[:, :key_dev] + row[:, key_dev:]
    n_copies = []
    for k in range(1, X):
        n_copies.append(x_copy(n_part, n_recv.at[k - 1], n_send_sem.at[k - 1], n_recv_sem.at[k - 1], k))
        n_copies[-1].start()

    load_i.wait()
    a_copies = []
    order = sorted(range(1, X), key=lambda k: -min(k, X - k)) + [0]
    for k in order:
        cols = pl.ds(pl.multiple_of(((t + k) % X) * cb, cb), cb)
        both = dot(pairs[...], i_ref[:, cols])
        a_part[k] = both[:key_dev] + both[key_dev:]
        if k:
            a_copies.append(x_copy(a_part.at[k], a_recv.at[k - 1], a_send_sem.at[k - 1], a_recv_sem.at[k - 1], k))
            a_copies[-1].start()

    count_row = jnp.concatenate([sc_ref[r : r + 1, :] for r in range(key_dev // LANES)], axis=1).astype(F32)
    count_wide = jnp.broadcast_to(count_row, (16, key_dev)).astype(BF16)
    item_row = dot(jnp.concatenate([count_wide, count_wide], axis=1), pairs[...])
    for r in range(item_dev // LANES):
        w_part[0, r : r + 1, :] = item_row[0:1, r * LANES : (r + 1) * LANES]

    def core_copy(src, dst, send, recv):
        return pltpu.make_async_remote_copy(
            src_ref=src, dst_ref=dst, send_sem=send, recv_sem=recv,
            device_id=(key(z, y, 1 - c), t), device_id_type=MESH,
        )

    def y_copy(src, dst, send, recv, k):
        return pltpu.make_async_remote_copy(
            src_ref=src, dst_ref=dst, send_sem=send, recv_sem=recv,
            device_id=(key(z, (y + k) % Y, c), t), device_id_type=MESH,
        )

    def z_copy(src, dst, send, recv, k, tile):
        return pltpu.make_async_remote_copy(
            src_ref=src, dst_ref=dst, send_sem=send, recv_sem=recv,
            device_id=(key((z + k) % Z, y, c), tile), device_id_type=MESH,
        )

    w_core = core_copy(w_part.at[0], w_recv.at[0], w_send_sem.at[0], w_recv_sem.at[0])
    w_core.start()

    load_s.wait()
    st = s_ref[...].T
    st_ref[...] = st.reshape(st_ref.shape)
    scaled[...] = (st * count_wide[0:1]).reshape(scaled.shape)

    def core_stage(kind, left, right):
        q_part[kind, 0] = dot(left(1 - c), right).reshape(q_part.shape[2:])
        copy = core_copy(q_part.at[kind, 0], q_recv.at[kind], q_send_sem.at[kind], q_recv_sem.at[kind])
        copy.start()
        q_part[kind, 1] = dot(left(c), right).reshape(q_part.shape[2:])
        return copy

    def y_stage(kind, copy):
        copy.wait()
        copies = []
        for k in list(range(1, Y)) + [0]:
            at = (y + k) % Y
            y_part[kind, k] = q_part[kind, 1, :, at] + q_recv[kind, :, at]
            if k:
                copies.append(
                    y_copy(
                        y_part.at[kind, k], y_recv.at[kind, k - 1],
                        y_send_sem.at[kind, k - 1], y_recv_sem.at[kind, k - 1], k,
                    )
                )
                copies[-1].start()
        return copies

    def z_stage(kind, copies):
        for copy in copies:
            copy.wait()
        tile = kind * (X // 2) + t // 2
        place = t % 2
        total = y_part[kind, 0]
        for k in range(1, Y):
            total += y_recv[kind, k - 1]
        z_part[kind] = total
        sends = []
        for k in range(Z):
            src = z_part.at[kind, (z + k) % Z]
            dst, recv = z_recv.at[place, k], z_recv_sem.at[place, k]
            copy = z_copy(src, dst, z_send_sem.at[kind, k], recv, k, tile)
            if k:
                copy.start()
                sends.append(copy)
            else:
                pl.when(tile != t)(copy.start)
                pl.when(tile == t)(pltpu.make_async_copy(src, dst, recv).start)
                sends.insert(0, copy)
        return tile, sends

    for copy in n_copies:
        copy.wait()
    store_row = n_part[...]
    for k in range(1, X):
        store_row += n_recv[k - 1]
    weight_row = count_row * store_row[0:1]

    def weighted(side):
        part = st_ref[:, :, side].reshape(-1, key_dev).astype(F32) * weight_row
        return split(part, 1)

    own = s_ref[:, pl.ds(pl.multiple_of(t * cb, cb), cb)]
    store_copy = core_stage(0, weighted, jnp.concatenate([own, own], axis=0))

    w_core.wait()
    w_part[1] = w_part[0] + w_recv[0]
    w_copies = []
    for k in range(1, Y):
        w_copies.append(y_copy(w_part.at[1], w_recv.at[k], w_send_sem.at[k], w_recv_sem.at[k], k))
        w_copies[-1].start()
    store_y = y_stage(0, store_copy)
    for copy in w_copies:
        copy.wait()
    total = w_part[1]
    for k in range(1, Y):
        total += w_recv[k]
    w_part[2] = total
    w_copies = []
    for k in range(1, Z):
        at = Y + k - 1
        w_copies.append(z_copy(w_part.at[2], w_recv.at[at], w_send_sem.at[at], w_recv_sem.at[at], k, t))
        w_copies[-1].start()
    store_tile, store_sends = z_stage(0, store_y)

    for copy in w_copies:
        copy.wait()
    total = w_part[2]
    for k in range(1, Z):
        total += w_recv[Y + k - 1]
    weights = jnp.concatenate([total[r : r + 1, :] for r in range(item_dev // LANES)], axis=1)
    wide = max(rows, LANES)
    block = i_ref[:, pl.ds(pl.multiple_of(((g * rows) // wide) * wide, wide), wide)]
    first = (g * rows) % wide
    pick = lax.broadcasted_iota(jnp.int32, (rows, wide), 1) == lax.broadcasted_iota(jnp.int32, (rows, wide), 0) + first
    picked = nt_dot(jnp.where(pick, 1.0, 0.0).astype(BF16), block)
    both = dot(split(picked * weights, 0), i_ref[...])
    item_rows = both[:rows] + both[rows:]
    for at in range(X):
        g_part[at, :rows] = item_rows[:, at * cb : (at + 1) * cb]
        g_part[at, rows:] = jnp.broadcast_to(jnp.sum(total), (8, cb))
    g_copies = []
    for k in range(1, X):
        g_copies.append(
            x_copy(g_part.at[(t + k) % X], g_recv.at[k - 1], g_send_sem.at[k - 1], g_recv_sem.at[k - 1], k)
        )
        g_copies[-1].start()

    for copy in a_copies:
        copy.wait()
    aggregate = a_part[0]
    for k in range(1, X):
        aggregate += a_recv[k - 1]

    def counted(side):
        part = scaled[:, :, side].reshape(-1, key_dev)
        return jnp.concatenate([part, part], axis=1)

    item_copy = core_stage(1, counted, split(aggregate, 0))
    item_y = y_stage(1, item_copy)
    item_tile, item_sends = z_stage(1, item_y)

    for copy in g_copies:
        copy.wait()
    item_rows = g_part[t]
    for k in range(1, X):
        item_rows += g_recv[k - 1]
    total = item_rows[rows : rows + 1]
    gram_ref[...] = item_rows[:rows] / total

    for place in range(2):
        for k in range(Z):
            z_copy(z_recv.at[place, k], z_recv.at[place, k], z_send_sem.at[0, k], z_recv_sem.at[place, k], k, t).wait_recv()
        block = z_recv[place, 0]
        for k in range(1, Z):
            block += z_recv[place, k]
        left_ref[:, place * cb : (place + 1) * cb] = block / total
    for tile, sends in ((store_tile, store_sends), (item_tile, item_sends)):
        pl.when(tile != t)(sends[0].wait_send)
        for copy in sends[1:]:
            copy.wait_send()


def shards(y_size, fact_store, fact_item, store_count, store_table, item_table):
    key_dev, width_a = store_table.shape
    item_dev, width_b = item_table.shape
    X = lax.axis_size("tiles")
    keys_count = lax.axis_size("keys")
    Y = y_size
    Z = keys_count // (CORES * Y)
    rows, cb = width_a // keys_count, width_b // X
    facts = fact_store.shape[0]
    vmem, dma = pltpu.VMEM, pltpu.SemaphoreType.DMA
    scratch = [
        vmem((key_dev, width_a), BF16), vmem((item_dev, width_b), BF16), dma((2,)),
        vmem((2 * key_dev, item_dev // 2), F32), vmem((2 * key_dev, item_dev), BF16),
        vmem((Z, Y, CORES, rows, key_dev), BF16), vmem((Z, Y, CORES, rows, key_dev), BF16),
        vmem((8, key_dev), F32), vmem((X - 1, 8, key_dev), F32), dma((X - 1,)), dma((X - 1,)),
        vmem((X, key_dev, cb), F32), vmem((X - 1, key_dev, cb), F32), dma((X - 1,)), dma((X - 1,)),
        vmem((2, 2, Z, Y, rows, cb), F32), vmem((2, Z, Y, rows, cb), F32), dma((2,)), dma((2,)),
        vmem((2, Y, Z, rows, cb), F32), vmem((2, Y - 1, Z, rows, cb), F32), dma((2, Y - 1)), dma((2, Y - 1)),
        vmem((2, Z, rows, cb), F32), vmem((2, Z, rows, cb), F32), dma((2, Z)), dma((2, Z)),
        vmem((3, 8, item_dev // 8), F32), vmem((Y + Z - 1, 8, item_dev // 8), F32),
        dma((Y + Z - 1,)), dma((Y + Z - 1,)),
        vmem((X, rows + 8, cb), F32), vmem((X - 1, rows + 8, cb), F32), dma((X - 1,)), dma((X - 1,)),
    ]
    whole = pl.BlockSpec(memory_space=pltpu.VMEM)
    anywhere = pl.BlockSpec(memory_space=pl.ANY)
    return pl.pallas_call(
        functools.partial(kernel, (X, Y, Z, key_dev, item_dev, cb, rows)),
        out_shape=[
            jax.ShapeDtypeStruct((rows, 2 * cb), F32),
            jax.ShapeDtypeStruct((rows, cb), F32),
        ],
        in_specs=[whole, whole, whole, anywhere, anywhere],
        out_specs=[whole, whole],
        scratch_shapes=scratch,
        compiler_params=pltpu.CompilerParams(
            collective_id=0, has_side_effects=True, vmem_limit_bytes=48 * 1024 * 1024
        ),
    )(
        fact_store.reshape(facts // LANES, LANES),
        fact_item.reshape(facts // LANES, LANES),
        store_count.reshape(key_dev // LANES, LANES),
        store_table,
        item_table,
    )


def solution(mesh, y_size=4):
    placed = (
        P(("keys", "tiles")),
        P(("keys", "tiles")),
        P("keys"),
        P("keys", None),
        P("tiles", None),
    )
    return jax.shard_map(
        functools.partial(shards, y_size),
        mesh=mesh,
        in_specs=placed,
        out_specs=(P("keys", "tiles"), P("keys", "tiles")),
        check_vma=False,
    )
```

time: 357 us -> 52.7 us (0.15)
  waiting for transfers between devices: 156 us -> 0 us
  blocking collectives: 141 us -> 0 us
  Pallas kernels: 0 us -> 45.8 us
  local copies, waits for them, and re-layouts: 26.3 us -> 5.96 us
  matrix products: 14.6 us -> 0 us
  between operations: 13.8 us -> 0.65 us
  other arithmetic: 5.07 us -> 0 us
    unnamed x4 -> x0, waiting for transfers between devices: 144 us -> none
    psum x2 -> x0, blocking collectives: 141 us -> none  [the longest x1 132 us: shards(): item_weight, total = lax.psum((item_weight, group_total), 'keys')]
    pallas_call x0 -> x1, Pallas kernels: none -> 45.8 us  [shards(): pl.pallas_call(functools.partial(kernel, (X, Y, Z, key_dev, item_dev, cb,...]
    gather x1 -> x0, local copies, waits for them, and re-layouts: 22.8 us -> none  [shards(): item_rows = jnp.take(item_table, local_item, axis=0)]
    dot_general x4 -> x0, matrix products: 14.6 us -> none  [the longest x1 6.88 us: shards(): jnp.dot(weighted.astype(jnp.bfloat16), item_rows, preferred_element_type=...]
    reduce_scatter x1 -> x0, waiting for transfers between devices: 11.6 us -> none  [shards(): lax.psum_scatter(partial_rows, 'tiles', scatter_dimension=1, tiled=True)]
  transfers between devices with their start and end apart: 3 -> 0, of which waited for: 2 -> 0; matrix products, arithmetic and copies ran while one was open for 4% -> 0% of each run, Pallas kernels for 0% -> 0%
where the time goes in v1:
time: 52.7 us; the launch traced here: 52.4 us
  Pallas kernels  45.8 us (87%)
  local copies, waits for them, and re-layouts  5.96 us (11%)
  between operations  0.65 us (1%)
    pallas_call x1, Pallas kernels, shards(): pl.pallas_call(functools.partial(kernel, (X, Y, Z, key_dev, item_dev, cb,...  45.8 us
    unnamed x12, local copies, waits for them, and re-layouts  5.96 us

profile of v1, /device:TPU:4, one launch (start us, length us, event | category | flops | bytes accessed | tf_op | source)
XLA Modules:
  0.0 52.4 jit_solution(785095403535653419)
XLA Ops:
  0.6 0.0 copy-start
  0.6 1.6 %copy-done = bf16[1024,1024]{1,0:T(8,128)(2,1)S(1)} copy-done((bf16[1024,1024]{1,0:T(8,128)(2,1)S(1)}, bf16[1024,1024]{1,0:T(8,128)(2,1)}, u32[]{:S(2)}) %copy-start) | copy-done | bytes 2097176
  2.2 0.0 copy-start.1
  2.2 1.0 %copy-done.1 = bf16[256,1024]{1,0:T(8,128)(2,1)S(1)} copy-done((bf16[256,1024]{1,0:T(8,128)(2,1)S(1)}, bf16[256,1024]{1,0:T(8,128)(2,1)}, u32[]{:S(2)}) %copy-start.1) | copy-done | bytes 524312
  3.3 0.0 copy-start.2
  3.3 0.7 %copy-done.2 = s32[4096]{0:T(1024)S(1)} copy-done((s32[4096]{0:T(1024)S(1)}, s32[4096]{0:T(1024)}, u32[]{:S(2)}) %copy-start.2) | copy-done | bytes 16408
  4.0 0.0 copy-start.3
  4.0 0.7 %copy-done.3 = s32[4096]{0:T(1024)S(1)} copy-done((s32[4096]{0:T(1024)S(1)}, s32[4096]{0:T(1024)}, u32[]{:S(2)}) %copy-start.3) | copy-done | bytes 16408
  4.7 0.0 copy-start.4
  4.7 0.7 %copy-done.4 = s32[256]{0:T(256)S(1)} copy-done((s32[256]{0:T(256)S(1)}, s32[256]{0:T(256)}, u32[]{:S(2)}) %copy-start.4) | copy-done | bytes 1048
  5.4 45.8 %shard_map.68 = (f32[16,512]{1,0:T(8,128)S(1)}, f32[16,256]{1,0:T(8,128)S(1)}) custom-call(s32[32,128]{1,0:T(8,128)S(1)} %bitcast.3, s32[32,128]{1,0:T(8,128)S(1)} %bitcast.4, s32[2,128]{1,0:T(2,128)S(1)} %bitcast.5, bf16[256,1024]{1,0:T(8,128)(2,1)S(1)} %copy-done.1, bf16[1024,1024]{1,0:T(8,128)(2,1)S(1)} %copy-done), custom_call_target="tpu_custom_call" | custom-call | tf_op jit(solution)/shard_map/pallas_call | solution.py:323
  51.2 0.6 %copy.9 = f32[16,512]{1,0:T(8,128)} copy(f32[16,512]{1,0:T(8,128)S(1)} %get-tuple-element.4) | data formatting | bytes 65536
  51.8 0.6 %copy.10 = f32[16,256]{1,0:T(8,128)} copy(f32[16,256]{1,0:T(8,128)S(1)} %get-tuple-element.5) | data formatting | bytes 32768
Async XLA Ops:
  0.6 1.6 %copy-start = (bf16[1024,1024]{1,0:T(8,128)(2,1)S(1)}, bf16[1024,1024]{1,0:T(8,128)(2,1)}, u32[]{:S(2)}) copy-start(bf16[1024,1024]{1,0:T(8,128)(2,1)} %i_hbm.1) | copy-start | bytes 6291460
  2.2 1.0 %copy-start.1 = (bf16[256,1024]{1,0:T(8,128)(2,1)S(1)}, bf16[256,1024]{1,0:T(8,128)(2,1)}, u32[]{:S(2)}) copy-start(bf16[256,1024]{1,0:T(8,128)(2,1)} %s_hbm.1) | copy-start | bytes 1572868
  3.3 0.7 %copy-start.2 = (s32[4096]{0:T(1024)S(1)}, s32[4096]{0:T(1024)}, u32[]{:S(2)}) copy-start(s32[4096]{0:T(1024)} %param.5) | copy-start | bytes 49156
  4.0 0.7 %copy-start.3 = (s32[4096]{0:T(1024)S(1)}, s32[4096]{0:T(1024)}, u32[]{:S(2)}) copy-start(s32[4096]{0:T(1024)} %param.6) | copy-start | bytes 49156
  4.7 0.7 %copy-start.4 = (s32[256]{0:T(256)S(1)}, s32[256]{0:T(256)}, u32[]{:S(2)}) copy-start(s32[256]{0:T(256)} %param.7) | copy-start | bytes 3076

commit v2 on v1

v2 whole, which is shorter than its diff:
```python
import functools

import jax
import jax.numpy as jnp
from jax import lax
from jax.experimental import pallas as pl
from jax.experimental.pallas import tpu as pltpu
from jax.sharding import PartitionSpec as P

MESH = pl.DeviceIdType.MESH
F32 = jnp.float32
BF16 = jnp.bfloat16
F8 = jnp.float8_e4m3fn
CORES = 2
LANES = 128


def nt_dot(a, b):
    return lax.dot_general(a, b, (((1,), (1,)), ((), ())), preferred_element_type=F32)


def dot(a, b):
    return jnp.dot(a, b, preferred_element_type=F32)


def split(x, axis):
    high = x.astype(BF16)
    low = (x - high.astype(F32)).astype(BF16)
    return jnp.concatenate([high, low], axis=axis)


def kernel(
    dims,
    fs_hbm, fi_hbm, sc_hbm, s_hbm, i_hbm,
    left_ref, gram_ref,
    fs_ref, fi_ref, sc_ref, s_ref, i_ref, in_sem,
    counts, pairs, st_ref, scaled,
    n_part, n_recv, n_send_sem, n_recv_sem,
    a_part, f_recv, a_recv, f_send_sem, f_recv_sem, a_send_sem, a_recv_sem,
    ss_bufs, sa0_bufs, sa1_bufs,
    w_part, w_recv, w_send_sem, w_recv_sem,
    g_part, g_recv, g_send_sem, g_recv_sem,
):
    X, Y, Z, key_dev, item_dev, cb, rows = dims
    g = lax.axis_index("keys")
    t = lax.axis_index("tiles")
    c = g % CORES
    y = (g // CORES) % Y
    z = g // (CORES * Y)

    def key(z_at, y_at, c_at):
        return (z_at * Y + y_at) * CORES + c_at

    loads = [
        pltpu.make_async_copy(src, dst, in_sem.at[n])
        for n, (src, dst) in enumerate(
            ((fs_hbm, fs_ref), (fi_hbm, fi_ref), (sc_hbm, sc_ref), (i_hbm, i_ref), (s_hbm, s_ref))
        )
    ]
    for load in loads:
        load.start()

    barrier = pltpu.get_barrier_semaphore()
    greeted = 0
    for dx in range(X):
        for dz in range(Z):
            if dx or dz:
                pl.semaphore_signal(
                    barrier, inc=1, device_id=(key((z + dz) % Z, y, c), (t + dx) % X), device_id_type=MESH
                )
                greeted += 1
    for dy in range(1, Y):
        pl.semaphore_signal(barrier, inc=1, device_id=(key(z, (y + dy) % Y, c), t), device_id_type=MESH)
        greeted += 1
    pl.semaphore_signal(barrier, inc=1, device_id=(key(z, y, 1 - c), t), device_id_type=MESH)
    greeted += 1

    loads[0].wait()
    loads[1].wait()
    half = item_dev // 2
    local_store = fs_ref[...] - g * key_dev
    local_item = fi_ref[...] - t * item_dev
    upper = jnp.where(local_item >= half, 1, 0)
    u = (upper * key_dev + local_store - 256).astype(F32)
    v = (local_item - upper * half - 256).astype(F32)
    iota = (lax.broadcasted_iota(jnp.int32, (512, LANES), 0) - 256).astype(F32).astype(BF16)
    iota = iota.reshape(32, 16, LANES)

    def hot(row):
        row = jnp.broadcast_to(row, (16, LANES)).astype(BF16)
        one = jnp.where(iota == row[None], jnp.ones((), BF16), jnp.zeros((), BF16))
        return one.reshape(512, LANES).astype(F8)

    per = 8
    for step in range(fs_ref.shape[0] // per):
        at = range(step * per, step * per + per)
        hot_u = jnp.concatenate([hot(u[r : r + 1]) for r in at], axis=1)
        hot_v = jnp.concatenate([hot(v[r : r + 1]) for r in at], axis=1)
        part = nt_dot(hot_u, hot_v)
        if step == 0:
            counts[...] = part
        else:
            counts[...] += part
    pairs[:, :half] = split(counts[:key_dev], 0)
    pairs[:, half:] = split(counts[key_dev:], 0)

    pl.semaphore_wait(barrier, greeted)

    def remote(src, dst, send, recv, at, tile):
        return pltpu.make_async_remote_copy(
            src_ref=src, dst_ref=dst, send_sem=send, recv_sem=recv, device_id=(at, tile), device_id_type=MESH
        )

    def x_copy(src, dst, send, recv, k):
        return remote(src, dst, send, recv, g, (t + k) % X)

    def core_copy(src, dst, send, recv):
        return remote(src, dst, send, recv, key(z, y, 1 - c), t)

    def y_copy(src, dst, send, recv, k):
        return remote(src, dst, send, recv, key(z, (y + k) % Y, c), t)

    def z_copy(src, dst, send, recv, k, tile):
        return remote(src, dst, send, recv, key((z + k) % Z, y, c), tile)

    ones = jnp.ones((8, item_dev), BF16)
    row = nt_dot(ones, pairs[...])
    n_part[...] = row[:, :key_dev] + row[:, key_dev:]
    n_copies = []
    for k in range(1, X):
        n_copies.append(x_copy(n_part, n_recv.at[k - 1], n_send_sem.at[k - 1], n_recv_sem.at[k - 1], k))
        n_copies[-1].start()

    steps = (1, X - 1)
    chunk = cb // 2
    pair = key_dev // 2

    def half_rows(n):
        return pl.ds(n * pair, pair)

    def forward(q, side):
        return x_copy(
            a_part.at[2, q, half_rows(side)], f_recv.at[side, q],
            f_send_sem.at[side, q], f_recv_sem.at[side, q], steps[side],
        )

    def direct(q, side, n):
        return x_copy(
            a_part.at[steps[side], q, half_rows(n)], a_recv.at[side, q, half_rows(n)],
            a_send_sem.at[side, q, n], a_recv_sem.at[side, q, n], steps[side],
        )

    def aggregate_block(k):
        cols = pl.ds(pl.multiple_of(((t + k) % X) * cb, cb), cb)
        both = dot(pairs[...], i_ref[:, cols])
        both = both[:key_dev] + both[key_dev:]
        for q in range(2):
            a_part[k, q] = both[:, q * chunk : (q + 1) * chunk]

    loads[3].wait()
    aggregate_block(2)
    for side in range(2):
        forward(0, side).start()
    for side in range(2):
        aggregate_block(steps[side])
        direct(0, side, 1 - side).start()
    aggregate_block(0)

    def pass_on(q):
        for side in range(2):
            forward(q, side).wait()
            a_part[steps[side], q, half_rows(side)] += f_recv[side, q]
            direct(q, side, side).start()

    loads[2].wait()
    count_row = jnp.concatenate([sc_ref[r : r + 1, :] for r in range(key_dev // LANES)], axis=1).astype(F32)
    count_wide = jnp.broadcast_to(count_row, (16, key_dev)).astype(BF16)
    item_row = dot(jnp.concatenate([count_wide, count_wide], axis=1), pairs[...])
    for r in range(item_dev // LANES):
        w_part[0, r : r + 1, :] = item_row[0:1, r * LANES : (r + 1) * LANES]
    w_core = core_copy(w_part.at[0], w_recv.at[0], w_send_sem.at[0], w_recv_sem.at[0])
    w_core.start()

    loads[4].wait()
    st = s_ref[...].T
    st_ref[...] = st.reshape(st_ref.shape)
    scaled[...] = (st * count_wide[0:1]).reshape(scaled.shape)

    pass_on(0)
    for side in range(2):
        forward(1, side).start()
    for side in range(2):
        direct(1, side, 1 - side).start()

    def core_stage(bufs, left, right):
        part, recv, send_sem, recv_sem = bufs[:4]
        part[0] = dot(left(1 - c), right).reshape(part.shape[1:])
        copy = core_copy(part.at[0], recv, send_sem, recv_sem)
        copy.start()
        part[1] = dot(left(c), right).reshape(part.shape[1:])

    def y_stage(bufs):
        part, recv, send_sem, recv_sem, y_part, y_recv, y_send_sem, y_recv_sem = bufs[:8]
        core_copy(part.at[0], recv, send_sem, recv_sem).wait()
        copies = []
        for k in (2, 1, 3, 0) if Y == 4 else list(range(1, Y)) + [0]:
            at = (y + k) % Y
            y_part[k] = part[1, :, at] + recv[:, at]
            if k:
                copies.append(
                    y_copy(y_part.at[k], y_recv.at[k - 1], y_send_sem.at[k - 1], y_recv_sem.at[k - 1], k)
                )
                copies[-1].start()
        return copies

    def z_stage(bufs, kind, copies):
        y_part, y_recv = bufs[4:6]
        z_part, z_recv, z_send_sem, z_recv_sem = bufs[8:]
        for copy in copies:
            copy.wait()
        tile = kind * (X // 2) + t // 2
        place = t % 2
        total = y_part[0]
        for k in range(1, Y):
            total += y_recv[k - 1]
        z_part[...] = total
        sends = []
        for k in sorted(range(Z), key=lambda k: -min(k, Z - k)):
            src = z_part.at[(z + k) % Z]
            dst, recv = z_recv.at[place, k], z_recv_sem.at[place, k]
            copy = z_copy(src, dst, z_send_sem.at[k], recv, k, tile)
            if k:
                copy.start()
            else:
                pl.when(tile != t)(copy.start)
                pl.when(tile == t)(pltpu.make_async_copy(src, dst, recv).start)
            sends.append(copy)

        def sent():
            for copy in sends[:-1]:
                copy.wait_send()
            pl.when(tile != t)(sends[-1].wait_send)

        return sent

    for copy in n_copies:
        copy.wait()
    store_row = n_part[...]
    for k in range(1, X):
        store_row += n_recv[k - 1]
    weight_row = count_row * store_row[0:1]

    def weighted(side):
        part = st_ref[:, :, side].reshape(-1, key_dev).astype(F32) * weight_row
        return split(part, 1)

    own = s_ref[:, pl.ds(pl.multiple_of(t * cb, cb), cb)]
    core_stage(ss_bufs, weighted, jnp.concatenate([own, own], axis=0))

    w_core.wait()
    w_part[1] = w_part[0] + w_recv[0]
    w_copies = []
    for k in range(1, Y):
        w_copies.append(y_copy(w_part.at[1], w_recv.at[k], w_send_sem.at[k], w_recv_sem.at[k], k))
        w_copies[-1].start()
    ss_y = y_stage(ss_bufs)

    pass_on(1)

    def counted(side):
        part = scaled[:, :, side].reshape(-1, key_dev)
        return jnp.concatenate([part, part], axis=1)

    def item_columns(q, bufs):
        for side in range(2):
            for n in range(2):
                direct(q, side, n).wait()
        core_stage(bufs, counted, split(a_part[0, q] + (a_recv[0, q] + a_recv[1, q]), 0))

    item_columns(0, sa0_bufs)

    for copy in w_copies:
        copy.wait()
    total = w_part[1]
    for k in range(1, Y):
        total += w_recv[k]
    w_part[2] = total
    w_copies = []
    for k in range(1, Z):
        at = Y + k - 1
        w_copies.append(z_copy(w_part.at[2], w_recv.at[at], w_send_sem.at[at], w_recv_sem.at[at], k, t))
        w_copies[-1].start()

    sa0_y = y_stage(sa0_bufs)
    item_columns(1, sa1_bufs)

    for copy in w_copies:
        copy.wait()
    total = w_part[2]
    for k in range(1, Z):
        total += w_recv[Y + k - 1]
    weights = jnp.concatenate([total[r : r + 1, :] for r in range(item_dev // LANES)], axis=1)
    wide = max(rows, LANES)
    block = i_ref[:, pl.ds(pl.multiple_of(((g * rows) // wide) * wide, wide), wide)]
    first = (g * rows) % wide
    pick = lax.broadcasted_iota(jnp.int32, (rows, wide), 1) == lax.broadcasted_iota(jnp.int32, (rows, wide), 0) + first
    picked = nt_dot(jnp.where(pick, 1.0, 0.0).astype(BF16), block)
    both = dot(split(picked * weights, 0), i_ref[...])
    item_rows = both[:rows] + both[rows:]
    for at in range(X):
        g_part[at, :rows] = item_rows[:, at * cb : (at + 1) * cb]
        g_part[at, rows:] = jnp.broadcast_to(jnp.sum(total), (8, cb))
    g_copies = []
    for k in range(1, X):
        g_copies.append(
            x_copy(g_part.at[(t + k) % X], g_recv.at[k - 1], g_send_sem.at[k - 1], g_recv_sem.at[k - 1], k)
        )
        g_copies[-1].start()

    sa1_y = y_stage(sa1_bufs)
    sents = [z_stage(ss_bufs, 0, ss_y)]
    sents.append(z_stage(sa0_bufs, 1, sa0_y))

    for copy in g_copies:
        copy.wait()
    item_rows = g_part[t]
    for k in range(1, X):
        item_rows += g_recv[k - 1]
    total = item_rows[rows : rows + 1, :chunk]
    gram_ref[...] = item_rows[:rows] / item_rows[rows : rows + 1]

    sents.append(z_stage(sa1_bufs, 1, sa1_y))

    def finish(bufs, col, divisor):
        z_recv, _, z_recv_sem = bufs[9:]
        width = z_recv.shape[-1]
        for place in range(2):
            for k in range(Z):
                z_copy(z_recv.at[place, k], z_recv.at[place, k], bufs[10].at[k], z_recv_sem.at[place, k], k, t).wait_recv()
            block = z_recv[place, 0]
            for k in range(1, Z):
                block += z_recv[place, k]
            left_ref[:, place * cb + col : place * cb + col + width] = block / divisor

    @pl.when(t < X // 2)
    def _():
        finish(ss_bufs, 0, item_rows[rows : rows + 1])

    @pl.when(t >= X // 2)
    def _():
        finish(sa0_bufs, 0, total)
        finish(sa1_bufs, chunk, total)

    for sent in sents:
        sent()


def shards(y_size, fact_store, fact_item, store_count, store_table, item_table):
    key_dev, width_a = store_table.shape
    item_dev, width_b = item_table.shape
    X = lax.axis_size("tiles")
    keys_count = lax.axis_size("keys")
    Y = y_size
    Z = keys_count // (CORES * Y)
    rows, cb = width_a // keys_count, width_b // X
    facts = fact_store.shape[0]
    vmem, dma = pltpu.VMEM, pltpu.SemaphoreType.DMA

    def reduction(width):
        return (
            vmem((2, Z, Y, rows, width), F32), vmem((Z, Y, rows, width), F32), dma(()), dma(()),
            vmem((Y, Z, rows, width), F32), vmem((Y - 1, Z, rows, width), F32), dma((Y - 1,)), dma((Y - 1,)),
            vmem((Z, rows, width), F32), vmem((2, Z, rows, width), F32), dma((Z,)), dma((2, Z)),
        )

    scratch = [
        vmem((facts // LANES, LANES), jnp.int32), vmem((facts // LANES, LANES), jnp.int32),
        vmem((key_dev // LANES, LANES), jnp.int32),
        vmem((key_dev, width_a), BF16), vmem((item_dev, width_b), BF16), dma((5,)),
        vmem((2 * key_dev, item_dev // 2), F32), vmem((2 * key_dev, item_dev), BF16),
        vmem((Z, Y, CORES, rows, key_dev), BF16), vmem((Z, Y, CORES, rows, key_dev), BF16),
        vmem((8, key_dev), F32), vmem((X - 1, 8, key_dev), F32), dma((X - 1,)), dma((X - 1,)),
        vmem((X, 2, key_dev, cb // 2), F32), vmem((2, 2, key_dev // 2, cb // 2), F32),
        vmem((2, 2, key_dev, cb // 2), F32), dma((2, 2)), dma((2, 2)), dma((2, 2, 2)), dma((2, 2, 2)),
        reduction(cb), reduction(cb // 2), reduction(cb // 2),
        vmem((3, 8, item_dev // 8), F32), vmem((Y + Z - 1, 8, item_dev // 8), F32),
        dma((Y + Z - 1,)), dma((Y + Z - 1,)),
        vmem((X, rows + 8, cb), F32), vmem((X - 1, rows + 8, cb), F32), dma((X - 1,)), dma((X - 1,)),
    ]
    whole = pl.BlockSpec(memory_space=pltpu.VMEM)
    hbm = pl.BlockSpec(memory_space=pltpu.HBM)
    return pl.pallas_call(
        functools.partial(kernel, (X, Y, Z, key_dev, item_dev, cb, rows)),
        out_shape=[
            jax.ShapeDtypeStruct((rows, 2 * cb), F32),
            jax.ShapeDtypeStruct((rows, cb), F32),
        ],
        in_specs=[hbm] * 5,
        out_specs=[whole, whole],
        scratch_shapes=scratch,
        compiler_params=pltpu.CompilerParams(
            collective_id=0, has_side_effects=True, vmem_limit_bytes=62 * 1024 * 1024
        ),
    )(
        fact_store.reshape(facts // LANES, LANES),
        fact_item.reshape(facts // LANES, LANES),
        store_count.reshape(key_dev // LANES, LANES),
        store_table,
        item_table,
    )


def solution(mesh, y_size=4):
    placed = (
        P(("keys", "tiles")),
        P(("keys", "tiles")),
        P("keys"),
        P("keys", None),
        P("tiles", None),
    )
    return jax.shard_map(
        functools.partial(shards, y_size),
        mesh=mesh,
        in_specs=placed,
        out_specs=(P("keys", "tiles"), P("keys", "tiles")),
        check_vma=False,
    )
```

time: 52.7 us -> 42.7 us (0.81)
  Pallas kernels: 45.8 us -> 38.8 us
  local copies, waits for them, and re-layouts: 5.96 us -> 2.7 us
    pallas_call x1, Pallas kernels: 45.8 us -> 38.8 us  [shards(): pl.pallas_call(functools.partial(kernel, (X, Y, Z, key_dev, item_dev, cb,...]
    unnamed x12 -> x2, local copies, waits for them, and re-layouts: 5.96 us -> 2.7 us
where the time goes in v2:
time: 42.7 us; the launch traced here: 42.2 us
  Pallas kernels  38.8 us (91%)
  local copies, waits for them, and re-layouts  2.7 us (6%)
  between operations  0.64 us (1%)
    pallas_call x1, Pallas kernels, shards(): pl.pallas_call(functools.partial(kernel, (X, Y, Z, key_dev, item_dev, cb,...  38.8 us
    unnamed x2, local copies, waits for them, and re-layouts  2.7 us

profile of v2, /device:TPU:4, one launch (start us, length us, event | category | flops | bytes accessed | tf_op | source)
XLA Modules:
  0.0 42.2 jit_solution(7283444115907764132)
XLA Ops:
  0.6 38.8 %shard_map.68 = (f32[16,512]{1,0:T(8,128)}, f32[16,256]{1,0:T(8,128)}) custom-call(s32[32,128]{1,0:T(8,128)} %bitcast.3, s32[32,128]{1,0:T(8,128)} %bitcast.4, s32[2,128]{1,0:T(2,128)} %bitcast.5, bf16[256,1024]{1,0:T(8,128)(2,1)} %s_hbm.1, bf16[1024,1024]{1,0:T(8,128)(2,1)} %i_hbm.1), custom_call_target="tpu_custom_call" | custom-call | tf_op jit(solution)/shard_map/pallas_call | solution.py:392
  39.5 1.4 %copy.9 = f32[16,512]{1,0:T(8,128)} copy(f32[16,512]{1,0:T(8,128)} %get-tuple-element.4) | data formatting | bytes 65536
  40.8 1.3 %copy.10 = f32[16,256]{1,0:T(8,128)} copy(f32[16,256]{1,0:T(8,128)} %get-tuple-element.5) | data formatting | bytes 32768

commit v3 on v2

--- a/solution.py
+++ b/solution.py
@@ -399,14 +399,19 @@
         out_specs=[whole, whole],
         scratch_shapes=scratch,
         compiler_params=pltpu.CompilerParams(
-            collective_id=0, has_side_effects=True, vmem_limit_bytes=62 * 1024 * 1024
+            collective_id=0, has_side_effects=True, vmem_limit_bytes=40 * 1024 * 1024
         ),
     )(
-        fact_store.reshape(facts // LANES, LANES),
-        fact_item.reshape(facts // LANES, LANES),
-        store_count.reshape(key_dev // LANES, LANES),
-        store_table,
-        item_table,
+        *(
+            pltpu.with_memory_space_constraint(operand, pltpu.HBM)
+            for operand in (
+                fact_store.reshape(facts // LANES, LANES),
+                fact_item.reshape(facts // LANES, LANES),
+                store_count.reshape(key_dev // LANES, LANES),
+                store_table,
+                item_table,
+            )
+        )
     )
 
 

time: 42.7 us -> 40.5 us (0.948)
  local copies, waits for them, and re-layouts: 2.7 us -> 1.22 us
  Pallas kernels: 38.8 us -> 38.2 us
    unnamed x2, local copies, waits for them, and re-layouts: 2.7 us -> 1.22 us
    pallas_call x1, Pallas kernels: 38.8 us -> 38.2 us  [shards(): pl.pallas_call(functools.partial(kernel, (X, Y, Z, key_dev, item_dev, cb,...]
where the time goes in v3:
time: 40.5 us; the launch traced here: 40.1 us
  Pallas kernels  38.2 us (94%)
  local copies, waits for them, and re-layouts  1.22 us (3%)
  between operations  0.64 us (2%)
    pallas_call x1, Pallas kernels, shards(): pl.pallas_call(functools.partial(kernel, (X, Y, Z, key_dev, item_dev, cb,...  38.2 us
    unnamed x2, local copies, waits for them, and re-layouts  1.22 us

profile of v3, /device:TPU:4, one launch (start us, length us, event | category | flops | bytes accessed | tf_op | source)
XLA Modules:
  0.0 40.1 jit_solution(16404575596327829388)
XLA Ops:
  0.6 38.2 %shard_map.68 = (f32[16,512]{1,0:T(8,128)S(1)}, f32[16,256]{1,0:T(8,128)S(1)}) custom-call(s32[32,128]{1,0:T(8,128)} %bitcast.3, s32[32,128]{1,0:T(8,128)} %bitcast.4, s32[2,128]{1,0:T(2,128)} %bitcast.5, bf16[256,1024]{1,0:T(8,128)(2,1)} %s_hbm.1, bf16[1024,1024]{1,0:T(8,128)(2,1)} %i_hbm.1), custom_call_target="tpu_custom_call" | custom-call | tf_op jit(solution)/shard_map/pallas_call | solution.py:392
  38.8 0.6 %copy.9 = f32[16,512]{1,0:T(8,128)} copy(f32[16,512]{1,0:T(8,128)S(1)} %get-tuple-element.4) | data formatting | bytes 65536
  39.5 0.6 %copy.10 = f32[16,256]{1,0:T(8,128)} copy(f32[16,256]{1,0:T(8,128)S(1)} %get-tuple-element.5) | data formatting | bytes 32768

commit v4 on v3

--- a/solution.py
+++ b/solution.py
@@ -48,6 +48,14 @@
     y = (g // CORES) % Y
     z = g // (CORES * Y)
 
+    def store_block(tile):
+        upper = tile // 2
+        return (1 - upper) * 2 * tile + upper * (7 - 2 * tile)
+
+    def item_block(tile):
+        upper = tile // 2
+        return (1 - upper) * (3 - 2 * tile) + upper * (2 * tile - 4)
+
     def key(z_at, y_at, c_at):
         return (z_at * Y + y_at) * CORES + c_at
 
@@ -151,7 +159,7 @@
         )
 
     def aggregate_block(k):
-        cols = pl.ds(pl.multiple_of(((t + k) % X) * cb, cb), cb)
+        cols = pl.ds(pl.multiple_of(item_block((t + k) % X) * cb, cb), cb)
         both = dot(pairs[...], i_ref[:, cols])
         both = both[:key_dev] + both[key_dev:]
         for q in range(2):
@@ -218,8 +226,9 @@
         z_part, z_recv, z_send_sem, z_recv_sem = bufs[8:]
         for copy in copies:
             copy.wait()
-        tile = kind * (X // 2) + t // 2
-        place = t % 2
+        block = item_block(t) if kind else store_block(t)
+        tile = kind * (X // 2) + block // 2
+        place = block % 2
         total = y_part[0]
         for k in range(1, Y):
             total += y_recv[k - 1]
@@ -254,7 +263,7 @@
         part = st_ref[:, :, side].reshape(-1, key_dev).astype(F32) * weight_row
         return split(part, 1)
 
-    own = s_ref[:, pl.ds(pl.multiple_of(t * cb, cb), cb)]
+    own = s_ref[:, pl.ds(pl.multiple_of(store_block(t) * cb, cb), cb)]
     core_stage(ss_bufs, weighted, jnp.concatenate([own, own], axis=0))
 
     w_core.wait()

time: 40.5 us -> 39.8 us (0.983)
  Pallas kernels: 38.2 us -> 37.5 us
    pallas_call x1, Pallas kernels: 38.2 us -> 37.5 us  [shards(): pl.pallas_call(functools.partial(kernel, (X, Y, Z, key_dev, item_dev, cb,...]
where the time goes in v4:
time: 39.8 us; the launch traced here: 39.3 us
  Pallas kernels  37.5 us (94%)
  local copies, waits for them, and re-layouts  1.22 us (3%)
  between operations  0.64 us (2%)
    pallas_call x1, Pallas kernels, shards(): pl.pallas_call(functools.partial(kernel, (X, Y, Z, key_dev, item_dev, cb,...  37.5 us
    unnamed x2, local copies, waits for them, and re-layouts  1.22 us

profile of v4, /device:TPU:4, one launch (start us, length us, event | category | flops | bytes accessed | tf_op | source)
XLA Modules:
  0.0 39.3 jit_solution(3397400200719909004)
XLA Ops:
  0.6 37.5 %shard_map.68 = (f32[16,512]{1,0:T(8,128)S(1)}, f32[16,256]{1,0:T(8,128)S(1)}) custom-call(s32[32,128]{1,0:T(8,128)} %bitcast.3, s32[32,128]{1,0:T(8,128)} %bitcast.4, s32[2,128]{1,0:T(2,128)} %bitcast.5, bf16[256,1024]{1,0:T(8,128)(2,1)} %s_hbm.1, bf16[1024,1024]{1,0:T(8,128)(2,1)} %i_hbm.1), custom_call_target="tpu_custom_call" | custom-call | tf_op jit(solution)/shard_map/pallas_call | solution.py:401
  38.1 0.6 %copy.9 = f32[16,512]{1,0:T(8,128)} copy(f32[16,512]{1,0:T(8,128)S(1)} %get-tuple-element.4) | data formatting | bytes 65536
  38.7 0.6 %copy.10 = f32[16,256]{1,0:T(8,128)} copy(f32[16,256]{1,0:T(8,128)S(1)} %get-tuple-element.5) | data formatting | bytes 32768

commit v5 on v4

--- a/solution.py
+++ b/solution.py
@@ -70,18 +70,12 @@
 
     barrier = pltpu.get_barrier_semaphore()
     greeted = 0
-    for dx in range(X):
-        for dz in range(Z):
-            if dx or dz:
-                pl.semaphore_signal(
-                    barrier, inc=1, device_id=(key((z + dz) % Z, y, c), (t + dx) % X), device_id_type=MESH
-                )
-                greeted += 1
-    for dy in range(1, Y):
-        pl.semaphore_signal(barrier, inc=1, device_id=(key(z, (y + dy) % Y, c), t), device_id_type=MESH)
+    partners = [(key(z, y, c), (t + dx) % X) for dx in range(1, X)] + [(key(z, y, 1 - c), t)]
+    partners += [(key(z, (y + dy) % Y, c), t) for dy in range(1, Y)]
+    partners += [(key((z + dz) % Z, y, c), (t + dx) % X) for dx in range(X) for dz in range(1, Z)]
+    for at, tile in partners:
+        pl.semaphore_signal(barrier, inc=1, device_id=(at, tile), device_id_type=MESH)
         greeted += 1
-    pl.semaphore_signal(barrier, inc=1, device_id=(key(z, y, 1 - c), t), device_id_type=MESH)
-    greeted += 1
 
     loads[0].wait()
     loads[1].wait()
@@ -99,14 +93,36 @@
         one = jnp.where(iota == row[None], jnp.ones((), BF16), jnp.zeros((), BF16))
         return one.reshape(512, LANES).astype(F8)
 
+    store_low = (local_store % LANES).astype(F32)
+    store_high = (local_store // LANES).astype(F32)
+    count = lax.broadcasted_iota(jnp.int32, (LANES, LANES), 0).astype(F32).astype(BF16).reshape(-1, 16, LANES)
+
+    def hot_store(row, groups):
+        row = jnp.broadcast_to(row, (16, LANES)).astype(BF16)
+        one = jnp.where(count[:groups] == row[None], jnp.ones((), BF16), jnp.zeros((), BF16))
+        return one.reshape(16 * groups, LANES)
+
+    steps = fs_ref.shape[0]
+    n_part[...] = nt_dot(
+        jnp.concatenate([hot_store(store_high[r : r + 1], 1) for r in range(steps)], axis=1),
+        jnp.concatenate([hot_store(store_low[r : r + 1], LANES // 16) for r in range(steps)], axis=1),
+    )
+
     per = 8
-    for step in range(fs_ref.shape[0] // per):
+    for step in range(steps // per):
         at = range(step * per, step * per + per)
         hot_u = jnp.concatenate([hot(u[r : r + 1]) for r in at], axis=1)
         hot_v = jnp.concatenate([hot(v[r : r + 1]) for r in at], axis=1)
         part = nt_dot(hot_u, hot_v)
         if step == 0:
             counts[...] = part
+            loads[2].wait()
+            loads[4].wait()
+            count_row = jnp.concatenate([sc_ref[r : r + 1, :] for r in range(key_dev // LANES)], axis=1).astype(F32)
+            count_wide = jnp.broadcast_to(count_row, (16, key_dev)).astype(BF16)
+            st = s_ref[...].T
+            st_ref[...] = st.reshape(st_ref.shape)
+            scaled[...] = (st * count_wide[0:1]).reshape(scaled.shape)
         else:
             counts[...] += part
     pairs[:, :half] = split(counts[:key_dev], 0)
@@ -131,15 +147,12 @@
     def z_copy(src, dst, send, recv, k, tile):
         return remote(src, dst, send, recv, key((z + k) % Z, y, c), tile)
 
-    ones = jnp.ones((8, item_dev), BF16)
-    row = nt_dot(ones, pairs[...])
-    n_part[...] = row[:, :key_dev] + row[:, key_dev:]
     n_copies = []
     for k in range(1, X):
         n_copies.append(x_copy(n_part, n_recv.at[k - 1], n_send_sem.at[k - 1], n_recv_sem.at[k - 1], k))
         n_copies[-1].start()
 
-    steps = (1, X - 1)
+    sides = (1, X - 1)
     chunk = cb // 2
     pair = key_dev // 2
 
@@ -149,13 +162,13 @@
     def forward(q, side):
         return x_copy(
             a_part.at[2, q, half_rows(side)], f_recv.at[side, q],
-            f_send_sem.at[side, q], f_recv_sem.at[side, q], steps[side],
+            f_send_sem.at[side, q], f_recv_sem.at[side, q], sides[side],
         )
 
     def direct(q, side, n):
         return x_copy(
-            a_part.at[steps[side], q, half_rows(n)], a_recv.at[side, q, half_rows(n)],
-            a_send_sem.at[side, q, n], a_recv_sem.at[side, q, n], steps[side],
+            a_part.at[sides[side], q, half_rows(n)], a_recv.at[side, q, half_rows(n)],
+            a_send_sem.at[side, q, n], a_recv_sem.at[side, q, n], sides[side],
         )
 
     def aggregate_block(k):
@@ -165,106 +178,30 @@
         for q in range(2):
             a_part[k, q] = both[:, q * chunk : (q + 1) * chunk]
 
+    def pass_on(q):
+        for side in range(2):
+            forward(q, side).wait()
+            a_part[sides[side], q, half_rows(side)] += f_recv[side, q]
+            direct(q, side, side).start()
+
     loads[3].wait()
     aggregate_block(2)
     for side in range(2):
         forward(0, side).start()
-    for side in range(2):
-        aggregate_block(steps[side])
-        direct(0, side, 1 - side).start()
-    aggregate_block(0)
-
-    def pass_on(q):
-        for side in range(2):
-            forward(q, side).wait()
-            a_part[steps[side], q, half_rows(side)] += f_recv[side, q]
-            direct(q, side, side).start()
-
-    loads[2].wait()
-    count_row = jnp.concatenate([sc_ref[r : r + 1, :] for r in range(key_dev // LANES)], axis=1).astype(F32)
-    count_wide = jnp.broadcast_to(count_row, (16, key_dev)).astype(BF16)
+
     item_row = dot(jnp.concatenate([count_wide, count_wide], axis=1), pairs[...])
     for r in range(item_dev // LANES):
         w_part[0, r : r + 1, :] = item_row[0:1, r * LANES : (r + 1) * LANES]
     w_core = core_copy(w_part.at[0], w_recv.at[0], w_send_sem.at[0], w_recv_sem.at[0])
     w_core.start()
 
-    loads[4].wait()
-    st = s_ref[...].T
-    st_ref[...] = st.reshape(st_ref.shape)
-    scaled[...] = (st * count_wide[0:1]).reshape(scaled.shape)
-
-    pass_on(0)
+    for side in range(2):
+        aggregate_block(sides[side])
+        direct(0, side, 1 - side).start()
     for side in range(2):
         forward(1, side).start()
-    for side in range(2):
         direct(1, side, 1 - side).start()
-
-    def core_stage(bufs, left, right):
-        part, recv, send_sem, recv_sem = bufs[:4]
-        part[0] = dot(left(1 - c), right).reshape(part.shape[1:])
-        copy = core_copy(part.at[0], recv, send_sem, recv_sem)
-        copy.start()
-        part[1] = dot(left(c), right).reshape(part.shape[1:])
-
-    def y_stage(bufs):
-        part, recv, send_sem, recv_sem, y_part, y_recv, y_send_sem, y_recv_sem = bufs[:8]
-        core_copy(part.at[0], recv, send_sem, recv_sem).wait()
-        copies = []
-        for k in (2, 1, 3, 0) if Y == 4 else list(range(1, Y)) + [0]:
-            at = (y + k) % Y
-            y_part[k] = part[1, :, at] + recv[:, at]
-            if k:
-                copies.append(
-                    y_copy(y_part.at[k], y_recv.at[k - 1], y_send_sem.at[k - 1], y_recv_sem.at[k - 1], k)
-                )
-                copies[-1].start()
-        return copies
-
-    def z_stage(bufs, kind, copies):
-        y_part, y_recv = bufs[4:6]
-        z_part, z_recv, z_send_sem, z_recv_sem = bufs[8:]
-        for copy in copies:
-            copy.wait()
-        block = item_block(t) if kind else store_block(t)
-        tile = kind * (X // 2) + block // 2
-        place = block % 2
-        total = y_part[0]
-        for k in range(1, Y):
-            total += y_recv[k - 1]
-        z_part[...] = total
-        sends = []
-        for k in sorted(range(Z), key=lambda k: -min(k, Z - k)):
-            src = z_part.at[(z + k) % Z]
-            dst, recv = z_recv.at[place, k], z_recv_sem.at[place, k]
-            copy = z_copy(src, dst, z_send_sem.at[k], recv, k, tile)
-            if k:
-                copy.start()
-            else:
-                pl.when(tile != t)(copy.start)
-                pl.when(tile == t)(pltpu.make_async_copy(src, dst, recv).start)
-            sends.append(copy)
-
-        def sent():
-            for copy in sends[:-1]:
-                copy.wait_send()
-            pl.when(tile != t)(sends[-1].wait_send)
-
-        return sent
-
-    for copy in n_copies:
-        copy.wait()
-    store_row = n_part[...]
-    for k in range(1, X):
-        store_row += n_recv[k - 1]
-    weight_row = count_row * store_row[0:1]
-
-    def weighted(side):
-        part = st_ref[:, :, side].reshape(-1, key_dev).astype(F32) * weight_row
-        return split(part, 1)
-
-    own = s_ref[:, pl.ds(pl.multiple_of(store_block(t) * cb, cb), cb)]
-    core_stage(ss_bufs, weighted, jnp.concatenate([own, own], axis=0))
+    aggregate_block(0)
 
     w_core.wait()
     w_part[1] = w_part[0] + w_recv[0]
@@ -272,22 +209,162 @@
     for k in range(1, Y):
         w_copies.append(y_copy(w_part.at[1], w_recv.at[k], w_send_sem.at[k], w_recv_sem.at[k], k))
         w_copies[-1].start()
-    ss_y = y_stage(ss_bufs)
-
-    pass_on(1)
-
-    def counted(side):
-        part = scaled[:, :, side].reshape(-1, key_dev)
-        return jnp.concatenate([part, part], axis=1)
-
-    def item_columns(q, bufs):
+
+    def core_stage(bufs, left, right):
+        part, recv, send_sem, recv_sem = bufs[:4]
+        part[0] = dot(left(1 - c), right).reshape(part.shape[1:])
+        copy = core_copy(part.at[0], recv, send_sem, recv_sem)
+        copy.start()
+
+    def own_stage(bufs, left, right):
+        bufs[0][1] = dot(left(c), right).reshape(bufs[1].shape)
+
+    def y_half(n):
+        return pl.ds(n * (Z // 2), Z // 2)
+
+    def y_forward(bufs, side):
+        y_part, f_recv, _, f_send_sem, f_recv_sem = bufs[4:9]
+        return y_copy(y_part.at[2, y_half(side)], f_recv.at[side], f_send_sem.at[side], f_recv_sem.at[side], sides[side])
+
+    def y_direct(bufs, side, n):
+        y_part, y_recv, y_send_sem, y_recv_sem = bufs[4], bufs[6], bufs[9], bufs[10]
+        return y_copy(
+            y_part.at[sides[side], y_half(n)], y_recv.at[side, y_half(n)],
+            y_send_sem.at[side, n], y_recv_sem.at[side, n], sides[side],
+        )
+
+    def y_begin(bufs):
+        part, recv, send_sem, recv_sem, y_part = bufs[:5]
+        core_copy(part.at[0], recv, send_sem, recv_sem).wait()
+
+        def add(k):
+            at = (y + k) % Y
+            y_part[k] = part[1, :, at] + recv[:, at]
+
+        add(2)
         for side in range(2):
-            for n in range(2):
-                direct(q, side, n).wait()
-        core_stage(bufs, counted, split(a_part[0, q] + (a_recv[0, q] + a_recv[1, q]), 0))
-
-    item_columns(0, sa0_bufs)
-
+            y_forward(bufs, side).start()
+        for side in range(2):
+            add(sides[side])
+            y_direct(bufs, side, 1 - side).start()
+        add(0)
+
+    def y_pass(bufs):
+        y_part, f_recv = bufs[4:6]
+        for side in range(2):
+            y_forward(bufs, side).wait()
+            y_part[sides[side], y_half(side)] += f_recv[side]
+            y_direct(bufs, side, side).start()
+
+    def y_end(bufs):
+        y_part, y_recv, z_part = bufs[4], bufs[6], bufs[11]
+        for side in range(2):
+            for n in (1 - side, side):
+                y_direct(bufs, side, n).wait()
+        z_part[...] = y_part[0] + (y_recv[0] + y_recv[1])
+
+    far_first = sorted(range(1, Z), key=lambda k: -min(k, Z - k))
+    place = item_block(t) % 2
+    store_place = store_block(t) % 2
+
+    def unless_here(tile, src, dst, send, recv, copy):
+        pl.when(tile != t)(copy.start)
+        pl.when(tile == t)(pltpu.make_async_copy(src, dst, recv).start)
+        return lambda: pl.when(tile != t)(copy.wait_send)
+
+    def z_own(bufs, k):
+        z_part, z_recv, z_send_sem, z_recv_sem = bufs[11:15]
+        return z_copy(z_part.at[(z + k) % Z], z_recv.at[0, k], z_send_sem.at[k], z_recv_sem.at[0, k], k, t)
+
+    def z_begin(bufs):
+        y_end(bufs)
+        for k in far_first:
+            z_own(bufs, k).start()
+
+    def z_end(bufs, kind):
+        z_part, z_recv = bufs[11:13]
+        part, recv, send_sem, recv_sem = bufs[15:]
+        for k in far_first:
+            z_own(bufs, k).wait()
+        block = z_part[z]
+        for k in range(1, Z):
+            block += z_recv[0, k]
+        part[...] = block
+        tile = kind * (X // 2) + (item_block(t) if kind else store_block(t)) // 2
+        copy = remote(part, recv.at[store_place], send_sem, recv_sem.at[store_place], g, tile)
+        return unless_here(tile, part, recv.at[store_place], send_sem, recv_sem.at[store_place], copy)
+
+    def landed(bufs, col, divisor):
+        _, recv, send_sem, recv_sem = bufs[15:]
+        width = recv.shape[-1]
+        for at in range(2):
+            remote(recv.at[at], recv.at[at], send_sem, recv_sem.at[at], g, t).wait_recv()
+            left_ref[:, at * cb + col : at * cb + col + width] = recv[at] / divisor
+
+    owner = X // 2 + item_block(t) // 2
+    near_first = sorted(range(1, Y), key=lambda k: -min(k, Y - k))
+
+    def item_y_copy(bufs, k):
+        y_part, y_recv, send_sem, recv_sem = bufs[4:8]
+        return y_copy(y_part.at[k], y_recv.at[k - 1], send_sem.at[k - 1], recv_sem.at[k - 1], k)
+
+    def item_y(bufs):
+        part, recv, send_sem, recv_sem, y_part = bufs[:5]
+        core_copy(part.at[0], recv, send_sem, recv_sem).wait()
+        for k in near_first + [0]:
+            at = (y + k) % Y
+            y_part[k] = part[1, :, at] + recv[:, at]
+            if k:
+                item_y_copy(bufs, k).start()
+
+    def item_z(bufs):
+        y_part, y_recv = bufs[4:6]
+        z_part, z_recv, z_send_sem, z_recv_sem = bufs[8:]
+        for k in near_first:
+            item_y_copy(bufs, k).wait()
+        block = y_part[0]
+        for k in range(1, Y):
+            block += y_recv[k - 1]
+        z_part[...] = block
+        sent = []
+        for k in far_first + [0]:
+            src, dst, send, got = z_part.at[(z + k) % Z], z_recv.at[place, k], z_send_sem.at[k], z_recv_sem.at[place, k]
+            copy = z_copy(src, dst, send, got, k, owner)
+            if k:
+                copy.start()
+                sent.append(copy.wait_send)
+            else:
+                sent.append(unless_here(owner, src, dst, send, got, copy))
+        return sent
+
+    def item_landed(bufs, col, divisor):
+        _, recv, send_sem, recv_sem = bufs[8:]
+        for at in range(2):
+            for k in range(Z):
+                slot = recv.at[at, k]
+                remote(slot, slot, send_sem.at[k], recv_sem.at[at, k], g, t).wait_recv()
+            block = recv[at, 0]
+            for k in range(1, Z):
+                block += recv[at, k]
+            left_ref[:, at * cb + col : at * cb + col + chunk] = block / divisor
+
+    for copy in n_copies:
+        copy.wait()
+    store_rows = n_part[...]
+    for k in range(1, X):
+        store_rows += n_recv[k - 1]
+    weight_row = count_row * jnp.concatenate([store_rows[r : r + 1] for r in range(key_dev // LANES)], axis=1)
+
+    def weighted(side):
+        part = st_ref[:, :, side].reshape(-1, key_dev).astype(F32) * weight_row
+        return split(part, 1)
+
+    own = s_ref[:, pl.ds(pl.multiple_of(store_block(t) * cb, cb), cb)]
+    own = jnp.concatenate([own, own], axis=0)
+    core_stage(ss_bufs, weighted, own)
+
+    pass_on(0)
+    own_stage(ss_bufs, weighted, own)
     for copy in w_copies:
         copy.wait()
     total = w_part[1]
@@ -300,8 +377,30 @@
         w_copies.append(z_copy(w_part.at[2], w_recv.at[at], w_send_sem.at[at], w_recv_sem.at[at], k, t))
         w_copies[-1].start()
 
-    sa0_y = y_stage(sa0_bufs)
+    y_begin(ss_bufs)
+
+    pass_on(1)
+    y_pass(ss_bufs)
+
+    def counted(side):
+        part = scaled[:, :, side].reshape(-1, key_dev)
+        return jnp.concatenate([part, part], axis=1)
+
+    def item_columns(q, bufs):
+        for side in range(2):
+            for n in range(2):
+                direct(q, side, n).wait()
+        right = split(a_part[0, q] + (a_recv[0, q] + a_recv[1, q]), 0)
+        core_stage(bufs, counted, right)
+        own_stage(bufs, counted, right)
+
+    item_columns(0, sa0_bufs)
+
+    item_y(sa0_bufs)
     item_columns(1, sa1_bufs)
+    item_y(sa1_bufs)
+    z_begin(ss_bufs)
+    sents = item_z(sa0_bufs)
 
     for copy in w_copies:
         copy.wait()
@@ -326,9 +425,8 @@
         )
         g_copies[-1].start()
 
-    sa1_y = y_stage(sa1_bufs)
-    sents = [z_stage(ss_bufs, 0, ss_y)]
-    sents.append(z_stage(sa0_bufs, 1, sa0_y))
+    sents.append(z_end(ss_bufs, 0))
+    sents += item_z(sa1_bufs)
 
     for copy in g_copies:
         copy.wait()
@@ -338,27 +436,14 @@
     total = item_rows[rows : rows + 1, :chunk]
     gram_ref[...] = item_rows[:rows] / item_rows[rows : rows + 1]
 
-    sents.append(z_stage(sa1_bufs, 1, sa1_y))
-
-    def finish(bufs, col, divisor):
-        z_recv, _, z_recv_sem = bufs[9:]
-        width = z_recv.shape[-1]
-        for place in range(2):
-            for k in range(Z):
-                z_copy(z_recv.at[place, k], z_recv.at[place, k], bufs[10].at[k], z_recv_sem.at[place, k], k, t).wait_recv()
-            block = z_recv[place, 0]
-            for k in range(1, Z):
-                block += z_recv[place, k]
-            left_ref[:, place * cb + col : place * cb + col + width] = block / divisor
-
     @pl.when(t < X // 2)
     def _():
-        finish(ss_bufs, 0, item_rows[rows : rows + 1])
+        landed(ss_bufs, 0, item_rows[rows : rows + 1])
 
     @pl.when(t >= X // 2)
     def _():
-        finish(sa0_bufs, 0, total)
-        finish(sa1_bufs, chunk, total)
+        item_landed(sa0_bufs, 0, total)
+        item_landed(sa1_bufs, chunk, total)
 
     for sent in sents:
         sent()
@@ -378,6 +463,15 @@
     def reduction(width):
         return (
             vmem((2, Z, Y, rows, width), F32), vmem((Z, Y, rows, width), F32), dma(()), dma(()),
+            vmem((Y, Z, rows, width), F32), vmem((2, Z // 2, rows, width), F32), vmem((2, Z, rows, width), F32),
+            dma((2,)), dma((2,)), dma((2, 2)), dma((2, 2)),
+            vmem((Z, rows, width), F32), vmem((1, Z, rows, width), F32), dma((Z,)), dma((1, Z)),
+            vmem((rows, width), F32), vmem((2, rows, width), F32), dma(()), dma((2,)),
+        )
+
+    def item_reduction(width):
+        return (
+            vmem((2, Z, Y, rows, width), F32), vmem((Z, Y, rows, width), F32), dma(()), dma(()),
             vmem((Y, Z, rows, width), F32), vmem((Y - 1, Z, rows, width), F32), dma((Y - 1,)), dma((Y - 1,)),
             vmem((Z, rows, width), F32), vmem((2, Z, rows, width), F32), dma((Z,)), dma((2, Z)),
         )
@@ -388,10 +482,10 @@
         vmem((key_dev, width_a), BF16), vmem((item_dev, width_b), BF16), dma((5,)),
         vmem((2 * key_dev, item_dev // 2), F32), vmem((2 * key_dev, item_dev), BF16),
         vmem((Z, Y, CORES, rows, key_dev), BF16), vmem((Z, Y, CORES, rows, key_dev), BF16),
-        vmem((8, key_dev), F32), vmem((X - 1, 8, key_dev), F32), dma((X - 1,)), dma((X - 1,)),
+        vmem((16, LANES), F32), vmem((X - 1, 16, LANES), F32), dma((X - 1,)), dma((X - 1,)),
         vmem((X, 2, key_dev, cb // 2), F32), vmem((2, 2, key_dev // 2, cb // 2), F32),
         vmem((2, 2, key_dev, cb // 2), F32), dma((2, 2)), dma((2, 2)), dma((2, 2, 2)), dma((2, 2, 2)),
-        reduction(cb), reduction(cb // 2), reduction(cb // 2),
+        reduction(cb), item_reduction(cb // 2), item_reduction(cb // 2),
         vmem((3, 8, item_dev // 8), F32), vmem((Y + Z - 1, 8, item_dev // 8), F32),
         dma((Y + Z - 1,)), dma((Y + Z - 1,)),
         vmem((X, rows + 8, cb), F32), vmem((X - 1, rows + 8, cb), F32), dma((X - 1,)), dma((X - 1,)),

time: 39.8 us -> 39.3 us (0.987)
  the two profiles are of different devices: /device:TPU:4 before, /device:TPU:6 now
where the time goes in v5:
time: 39.3 us; the launch traced here: 39.1 us
  Pallas kernels  37.3 us (95%)
  local copies, waits for them, and re-layouts  1.22 us (3%)
  between operations  0.64 us (2%)
    pallas_call x1, Pallas kernels, shards(): pl.pallas_call(functools.partial(kernel, (X, Y, Z, key_dev, item_dev, cb,...  37.3 us
    unnamed x2, local copies, waits for them, and re-layouts  1.22 us

profile of v5, /device:TPU:6, one launch (start us, length us, event | category | flops | bytes accessed | tf_op | source)
XLA Modules:
  0.0 39.1 jit_solution(7232143251797892062)
XLA Ops:
  0.6 37.3 %shard_map.68 = (f32[16,512]{1,0:T(8,128)S(1)}, f32[16,256]{1,0:T(8,128)S(1)}) custom-call(s32[32,128]{1,0:T(8,128)} %bitcast.3, s32[32,128]{1,0:T(8,128)} %bitcast.4, s32[2,128]{1,0:T(2,128)} %bitcast.5, bf16[256,1024]{1,0:T(8,128)(2,1)} %s_hbm.1, bf16[1024,1024]{1,0:T(8,128)(2,1)} %i_hbm.1), custom_call_target="tpu_custom_call" | custom-call | tf_op jit(solution)/shard_map/pallas_call | solution.py:495
  37.9 0.6 %copy.9 = f32[16,512]{1,0:T(8,128)} copy(f32[16,512]{1,0:T(8,128)S(1)} %get-tuple-element.4) | data formatting | bytes 65536
  38.5 0.6 %copy.10 = f32[16,256]{1,0:T(8,128)} copy(f32[16,256]{1,0:T(8,128)S(1)} %get-tuple-element.5) | data formatting | bytes 32768

commit v6 on v5

--- a/solution.py
+++ b/solution.py
@@ -399,9 +399,6 @@
     item_y(sa0_bufs)
     item_columns(1, sa1_bufs)
     item_y(sa1_bufs)
-    z_begin(ss_bufs)
-    sents = item_z(sa0_bufs)
-
     for copy in w_copies:
         copy.wait()
     total = w_part[2]
@@ -424,6 +421,8 @@
             x_copy(g_part.at[(t + k) % X], g_recv.at[k - 1], g_send_sem.at[k - 1], g_recv_sem.at[k - 1], k)
         )
         g_copies[-1].start()
+    z_begin(ss_bufs)
+    sents = item_z(sa0_bufs)
 
     sents.append(z_end(ss_bufs, 0))
     sents += item_z(sa1_bufs)

time: 39.3 us -> 39.3 us (level)
  no operation moved by 1% of the time
where the time goes in v6:
time: 39.3 us; the launch traced here: 39.1 us
  Pallas kernels  37.3 us (95%)
  local copies, waits for them, and re-layouts  1.22 us (3%)
  between operations  0.64 us (2%)
    pallas_call x1, Pallas kernels, shards(): pl.pallas_call(functools.partial(kernel, (X, Y, Z, key_dev, item_dev, cb,...  37.3 us
    unnamed x2, local copies, waits for them, and re-layouts  1.22 us

profile of v6, /device:TPU:6, one launch (start us, length us, event | category | flops | bytes accessed | tf_op | source)
XLA Modules:
  0.0 39.1 jit_solution(6466216635177713323)
XLA Ops:
  0.6 37.3 %shard_map.68 = (f32[16,512]{1,0:T(8,128)S(1)}, f32[16,256]{1,0:T(8,128)S(1)}) custom-call(s32[32,128]{1,0:T(8,128)} %bitcast.3, s32[32,128]{1,0:T(8,128)} %bitcast.4, s32[2,128]{1,0:T(2,128)} %bitcast.5, bf16[256,1024]{1,0:T(8,128)(2,1)} %s_hbm.1, bf16[1024,1024]{1,0:T(8,128)(2,1)} %i_hbm.1), custom_call_target="tpu_custom_call" | custom-call | tf_op jit(solution)/shard_map/pallas_call | solution.py:494
  37.9 0.6 %copy.9 = f32[16,512]{1,0:T(8,128)} copy(f32[16,512]{1,0:T(8,128)S(1)} %get-tuple-element.4) | data formatting | bytes 65536
  38.5 0.6 %copy.10 = f32[16,256]{1,0:T(8,128)} copy(f32[16,256]{1,0:T(8,128)S(1)} %get-tuple-element.5) | data formatting | bytes 32768
